TPU v7x, 32 devices: a whole 2x2x4 slice. The times are simulated.
32 devices in a mesh: ctx: 4 (over y, x), head: 2 (over core), dp: 4 (over z).
Axes of the slice: x: 2, y: 2, z: 4, core: 2. Of those that a mesh axis runs over, the one named last changes fastest.
Arguments:
- query_raw: bfloat16 [4, 512, 4096], P('dp', 'ctx', 'head'), may hold values from -6 to 6
- key_raw: bfloat16 [4, 512, 512], P('dp', 'ctx', 'head'), may hold values from -6 to 6
- value_rows: bfloat16 [4, 512, 512], P('dp', 'ctx', 'head'), may hold values from -6 to 6
- attn_out: bfloat16 [4, 512, 4096], P('dp', 'ctx', 'head'), may hold values from -2 to 2
- out_grad: bfloat16 [4, 512, 4096], P('dp', 'ctx', 'head'), may hold values from -6 to 6
- log_totals: float32 [4, 32, 512], P('dp', 'head', 'ctx'), may hold values from -40 to 40, as said below
- query_gain: float32 [128], replicated, may hold values from 0.5 to 1.5
- key_gain: float32 [128], replicated, may hold values from 0.5 to 1.5
Outputs:
- grad_query: float32 [4, 512, 4096], P('dp', 'ctx', 'head')
- grad_key: float32 [4, 512, 512], P('dp', 'ctx', 'head')
- grad_value: float32 [4, 512, 512], P('dp', 'ctx', 'head')
- gain_grads: float32 [2, 128], replicated
Inputs may be any that keep to these rules, and one draw needn't show every extreme that they name: log_totals[s, h, i] is the log of the sum over j <= i of exp(score[i, j]) for query head h, computed from query_raw, key_raw and the gains.
All inputs are finite; a program needn't handle non-finite values.
Results may differ from a plain program's by a relative error of at most 0.009.
Values may be sent and summed in bfloat16 or wider, within the bound.
A program may use at most 64 MiB of HBM per device.

v0:
```python
import math

import jax
import jax.numpy as jnp
from jax import lax
from jax.sharding import PartitionSpec as P

HD = 128


def normalize(raw_rows, norm_gain):
    values = raw_rows.astype(jnp.float32).reshape(raw_rows.shape[:-1] + (-1, HD))
    inverse = lax.rsqrt(jnp.mean(values * values, axis=-1, keepdims=True) + 1e-06)
    unit_rows = values * inverse
    return (unit_rows, inverse, (unit_rows * norm_gain).astype(jnp.bfloat16))


def norm_back(grad_norm, unit_rows, inverse, norm_gain):
    grad_unit = grad_norm * norm_gain
    grad_raw = (
        grad_unit - unit_rows * jnp.mean(grad_unit * unit_rows, axis=-1, keepdims=True)
    ) * inverse
    return (grad_raw, jnp.sum(grad_norm * unit_rows, axis=(0, 1)))


def rounded_values(values):
    return lax.optimization_barrier(values.astype(jnp.bfloat16)).astype(jnp.float32)


def local(query_raw, key_raw, value_rows, attn_out, out_grad, log_totals, query_gain, key_gain):
    rows = query_raw.shape[1]
    width = query_raw.shape[2]
    kv_width = key_raw.shape[2]
    head_count = width // HD
    kv_count = kv_width // HD
    group = head_count // kv_count
    block_count = lax.axis_size("ctx")
    block_index = lax.axis_index("ctx")
    group_size = math.gcd(block_count, 4)
    step_count = block_count // group_size
    logit_scale = 1.0 / math.sqrt(HD)
    local_rows = jnp.arange(rows)
    query_list, key_list, value_list = ([], [], [])
    q_unit, q_inverse, q_norm = normalize(query_raw[0], query_gain)
    k_unit, k_inverse, k_norm = normalize(key_raw[0], key_gain)
    k_flat = k_norm.reshape(rows, kv_width)
    v_flat = value_rows[0]
    g_flat = out_grad[0]
    delta = jnp.einsum(
        "thd,thd->ht",
        g_flat.reshape(rows, head_count, HD),
        attn_out[0].reshape(rows, head_count, HD),
        preferred_element_type=jnp.float32,
    )
    delta_groups = delta.reshape(kv_count, group, rows)
    total_groups = log_totals[0].reshape(kv_count, group, rows)
    gathered = (
        lax.all_gather(k_flat, "ctx", axis=0, tiled=True),
        lax.all_gather(v_flat, "ctx", axis=0, tiled=True),
    )
    key_steps = gathered[0].reshape(step_count, group_size, rows, kv_count, HD)
    value_steps = gathered[1].reshape(step_count, group_size, rows, kv_count, HD)
    q_heads = q_norm.reshape(rows, kv_count, group, HD)
    g_heads = g_flat.reshape(rows, kv_count, group, HD)
    query_pos = block_index * rows + local_rows

    def key_step(running, inputs):
        key_group, value_group, step_index = inputs
        key_pos = step_index * group_size * rows + jnp.arange(group_size * rows).reshape(
            group_size, rows
        )
        attention_logits = (
            jnp.einsum("qcgd,pkcd->cgqpk", q_heads, key_group, preferred_element_type=jnp.float32)
            * logit_scale
        )
        causal = query_pos[:, None, None] >= key_pos[None]
        probs = jnp.where(
            causal[None, None], jnp.exp(attention_logits - total_groups[:, :, :, None, None]), 0.0
        )
        probs_low = probs.astype(jnp.bfloat16)
        value_part = jnp.einsum(
            "cgqpk,qcgd->pkcd", probs_low, g_heads, preferred_element_type=jnp.float32
        ).astype(jnp.bfloat16)
        probability_gradient = jnp.einsum(
            "qcgd,pkcd->cgqpk", g_heads, value_group, preferred_element_type=jnp.float32
        )
        score_gradient = (
            probs * (probability_gradient - delta_groups[:, :, :, None, None])
        ).astype(jnp.bfloat16)
        query_part = rounded_values(
            jnp.einsum(
                "cgqpk,pkcd->pqcgd", score_gradient, key_group, preferred_element_type=jnp.float32
            )
            * logit_scale
        )
        key_part = (
            jnp.einsum(
                "cgqpk,qcgd->pkcd", score_gradient, q_heads, preferred_element_type=jnp.float32
            )
            * logit_scale
        ).astype(jnp.bfloat16)
        return (running + jnp.sum(query_part, axis=0), (key_part, value_part))

    grad_q_groups, parts = lax.scan(
        key_step,
        jnp.zeros((rows, kv_count, group, HD), jnp.float32),
        (key_steps, value_steps, jnp.arange(step_count)),
    )
    grad_q_norm = grad_q_groups.reshape(rows, head_count, HD)
    terms = jnp.concatenate(
        [
            parts[0].reshape(block_count * rows, kv_width),
            parts[1].reshape(block_count * rows, kv_width),
        ],
        axis=1,
    )
    received = lax.all_to_all(
        terms.reshape(block_count, rows, 2 * kv_width),
        "ctx",
        split_axis=0,
        concat_axis=0,
        tiled=True,
    )
    summed = jnp.sum(received.astype(jnp.float32), axis=0)
    grad_k_norm = summed[:, :kv_width].reshape(rows, kv_count, HD)
    grad_value = summed[:, kv_width:]
    grad_query, q_sum = norm_back(grad_q_norm, q_unit, q_inverse, query_gain)
    grad_key, k_sum = norm_back(grad_k_norm, k_unit, k_inverse, key_gain)
    query_list.append(grad_query.reshape(rows, width))
    key_list.append(grad_key.reshape(rows, kv_width))
    value_list.append(grad_value)
    summed_gains = lax.psum(jnp.stack([q_sum, k_sum]), ("ctx", "head", "dp"))
    pair_count = (
        query_raw.shape[0]
        * lax.axis_size("dp")
        * rows
        * block_count
        * head_count
        * lax.axis_size("head")
    )
    gain_grads = summed_gains * (1.0 / math.sqrt(pair_count))
    return (jnp.stack(query_list), jnp.stack(key_list), jnp.stack(value_list), gain_grads)


def solution(mesh):
    return jax.shard_map(
        local,
        mesh=mesh,
        in_specs=(
            P("dp", "ctx", "head"),
            P("dp", "ctx", "head"),
            P("dp", "ctx", "head"),
            P("dp", "ctx", "head"),
            P("dp", "ctx", "head"),
            P("dp", "head", "ctx"),
            P(),
            P(),
        ),
        out_specs=(P("dp", "ctx", "head"), P("dp", "ctx", "head"), P("dp", "ctx", "head"), P()),
        check_vma=False,
    )
```

profile of v0, /device:TPU:0, one launch (start us, length us, event | category | flops | bytes accessed | tf_op | source)
XLA Modules:
  0.0 97.5 jit_solution(8390919611349570197)
XLA Ops:
  0.7 0.6 multiply_add_fusion
  1.2 1.1 %multiply_bitcast_fusion = f32[16,8,16,128]{3,1,2,0:T(8,128)S(1)} fusion(bf16[1,128,2048]{2,1,0:T(8,128)(2,1)} %param.8), kind=kLoop, calls=%fused_computation.27 | loop fusion | flops 524288 | bytes 1572864
  2.4 1.2 %copy.146 = f32[1,128,2048]{1,2,0:T(8,128)S(1)} copy(bf16[1,128,2048]{2,1,0:T(8,128)(2,1)} %param.8) | data formatting | bytes 1572864 | tf_op jit(solution)/shard_map/convert_element_type | solution.py:12
  3.6 0.6 iota_add_fusion
  4.2 0.7 broadcast_bitcast_fusion.1
  4.9 0.9 copy.99
  5.8 0.7 multiply_reduce_fusion.4
  6.6 10.4 %all_gather.6 = bf16[512,256]{0,1:T(8,128)(2,1)S(1)} all-gather(bf16[128,256]{0,1:T(8,128)(2,1)S(1)} %multiply_convert_fusion.2), channel_id=1, replica_groups=mesh['ctx'=4,'head'=2,'dp'=4] {'ctx'}, dimensions={0}, use_global_device_ids=true | all-gather | bytes 327680 | tf_op jit(solution)/shard_map/all_gather | solution.py:58
  17.2 9.0 %all-gather = bf16[1,512,256]{2,1,0:T(8,128)(2,1)S(1)} all-gather(bf16[1,128,256]{2,1,0:T(8,128)(2,1)S(1)} %copy-done.6), channel_id=2, replica_groups=mesh['ctx'=4,'head'=2,'dp'=4] {'ctx'}, dimensions={1}, use_global_device_ids=true | all-gather | bytes 327680 | tf_op jit(solution)/shard_map/all_gather | solution.py:59
  26.1 0.8 squeeze.19
  27.0 1.2 %copy.137 = bf16[128,2,8,128,1]{0,3,2,4,1:T(8,128)(2,1)} copy(bf16[128,2,8,128,1]{3,2,1,0,4:T(8,128)(2,1)S(1)} %bitcast.139) | data formatting | bytes 1048576 | tf_op jit(solution)/shard_map/reshape;squeeze | solution.py:64
  28.2 1.1 %copy.162 = bf16[16,8,16,128]{3,2,1,0:T(8,128)(2,1)S(1)} copy(bf16[16,8,16,128]{3,1,2,0:T(8,128)(2,1)} %bitcast.150) | data formatting | bytes 1048576
  29.4 0.4 fusion.24
  30.0 0.3 reduce_sum.88
  30.4 0.8 broadcast_compare_fusion
  31.3 0.8 fusion.27
  32.1 1.0 %fusion.21 = bf16[4,128,2,128]{1,3,0,2:T(8,128)(2,1)S(1)} fusion(bf16[128,2,8,128,1]{0,3,2,4,1:T(8,128)(2,1)S(1)} %copy-done.2, f32[2,4,128,128,8]{3,2,4,1,0:T(8,128)S(1)} %fusion.27, f32[2,8,128]{2,1,0:T(8,128)S(1)} %bitcast.155, pred[128,4,128]{0,2,1:T(8,128)(4,1)S(1)} %broadcast_compare_fusion), kind=kOutput, calls=%fused_computation.19 | convolution fusion | flops 272760832 | bytes 5054464 | tf_op jit(solution)/shard_map/while/body/eval_jaxpr/cgqpk,qcgd->pkcd/dot_general | solution.py:81
  33.2 1.3 %fusion.1 = bf16[2,8,128,4,128]{2,4,1,3,0:T(8,128)(2,1)S(1)} fusion(f32[2,4,128,128,8]{3,2,4,1,0:T(8,128)S(1)} %fusion.27, bf16[128,2,8,128,1]{0,3,2,4,1:T(8,128)(2,1)S(1)} %copy-done.3, f32[2,8,128]{2,1,0:T(8,128)S(1)} %bitcast.152, f32[2,8,128]{2,1,0:T(8,128)S(1)} %bitcast.156, pred[128,4,128]{0,2,1:T(8,128)(4,1)S(1)} %broadcast_compare_fusion, ...), kind=kOutput, calls=%fused_computation.2 | convolution fusion | flops 274726912 | bytes 7159808 | tf_op jit(solution)/shard_map/while/body/eval_jaxpr/qcgd,pkcd->cgqpk/dot_general | solution.py:84
  34.5 0.8 fusion.20
  35.4 0.9 pad_maximum_fusion
  36.2 4.1 %all-to-all-start = ((bf16[4,128,512]{1,2,0:T(8,128)(2,1)}), bf16[4,128,512]{1,2,0:T(8,128)(2,1)}, u32[]{:S(2)}, u32[]{:S(2)}) async-start(bf16[4,128,512]{1,2,0:T(8,128)(2,1)} %pad_maximum_fusion), calls=%async_computation | async-start | bytes 1048576 | tf_op jit(solution)/shard_map/all_to_all | solution.py:117
  40.4 2.1 %fusion.9 = bf16[4,128,2,8,128]{1,4,3,2,0:T(8,128)(2,1)} fusion(bf16[2,8,128,4,128]{2,4,1,3,0:T(8,128)(2,1)S(1)} %fusion.1, bf16[4,128,2,128,1]{1,0,3,2,4:T(4,128)(2,1)S(1)} %bitcast.144), kind=kOutput, calls=%fused_computation.12 | convolution fusion | flops 270532608 | bytes 4456448 | tf_op jit(solution)/shard_map/while/body/eval_jaxpr/cgqpk,pkcd->pqcgd/dot_general | solution.py:91
  42.9 1.1 %mul.236 = f32[1,128,2048]{2,1,0:T(8,128)} reshape(f32[128,16,128]{2,1,0:T(8,128)S(1)} %mul.235) | data formatting | bytes 2097152 | tf_op jit(solution)/shard_map/mul | solution.py:14
  44.1 1.3 %copy.158 = f32[1,128,2048]{2,1,0:T(8,128)} copy(f32[1,128,2048]{1,2,0:T(8,128)S(1)} %bitcast.142) | data formatting | bytes 2097152 | tf_op jit(solution)/shard_map/mul | solution.py:14
  45.4 2.1 %convert_reduce_fusion = f32[128,2,8,128]{0,3,2,1:T(8,128)S(1)} fusion(bf16[4,128,2,8,128]{1,4,3,2,0:T(8,128)(2,1)} %fusion.9), kind=kLoop, calls=%fused_computation.6 | loop fusion | flops 1835008 | bytes 3145728 | tf_op jit(solution)/shard_map/while/body/eval_jaxpr/reduce_sum | solution.py:102
  47.8 1.3 %copy.155 = f32[1,128,2048]{2,1,0:T(8,128)} copy(f32[1,128,2048]{1,2,0:T(8,128)S(1)} %bitcast.138) | data formatting | bytes 2097152 | tf_op jit(solution)/shard_map/reshape | solution.py:109
  49.7 3.3 %multiply_reduce_fusion = (f32[2048]{0:T(1024)S(1)}, f32[1,128,2048]{2,1,0:T(8,128)}) fusion(f32[1,128,2048]{2,1,0:T(8,128)} %copy.155, f32[1,128,2048]{2,1,0:T(8,128)} %copy.158, bf16[1,128,2048]{2,1,0:T(8,128)(2,1)S(1)} %copy-done, f32[1,128,2048]{2,1,0:T(8,128)} %mul.236, f32[1,128,2048]{2,1,0:T(8,128)S(1)} %mul.241, f32[2048]{0:T(1024)S(1)} %broadcast_bitcast_fusion), kind=kLoop, calls=%fused_computation.22 | loop fusion | flops 2357248 | bytes 5783552 | tf_op jit(solution)/shard_map/reduce_sum | solution.py:23
  53.0 1.1 %convert_reduce_fusion.1 = f32[128,512]{0,1:T(8,128)S(1)} fusion(bf16[4,128,512]{1,2,0:T(8,128)(2,1)} %all-to-all-done), kind=kLoop, calls=%fused_computation.23 | loop fusion | flops 458752 | bytes 786432 | tf_op jit(solution)/shard_map/reduce_sum | solution.py:124
  54.6 0.8 copy.118
  55.3 0.8 copy.119
  56.1 40.9 %psum.7 = f32[2,128]{1,0:T(2,128)S(1)} all-reduce(f32[2,128]{1,0:T(2,128)S(1)} %pad_maximum_fusion.1), channel_id=1, replica_groups=mesh['ctx'=4,'head'=2,'dp'=4] {'ctx','head','dp'}, use_global_device_ids=true, to_apply=%region_10.11 | all-reduce | flops 256 | bytes 2048 | tf_op jit(solution)/shard_map/psum | solution.py:132
  96.9 0.6 broadcast_multiply_fusion
  (51 shorter events, 2.5 us)
Async XLA Ops:
  0.6 16.5 %copy-start.6 = (bf16[1,128,256]{2,1,0:T(8,128)(2,1)S(1)}, bf16[1,128,256]{2,1,0:T(8,128)(2,1)}, u32[]{:S(2)}) copy-start(bf16[1,128,256]{2,1,0:T(8,128)(2,1)} %param.10) | copy-start | bytes 196612
  0.6 26.2 %copy-start.1 = (bf16[1,128,2048]{2,1,0:T(8,128)(2,1)S(1)}, bf16[1,128,2048]{2,1,0:T(8,128)(2,1)}, u32[]{:S(2)}) copy-start(bf16[1,128,2048]{2,1,0:T(8,128)(2,1)} %param.12) | copy-start | bytes 1572868
  4.9 24.5 %copy-start.8 = (f32[256]{0:T(256)}, f32[256]{0:T(256)S(1)}, u32[]{:S(2)}) copy-start(f32[256]{0:T(256)S(1)} %broadcast_bitcast_fusion.1) | copy-start | bytes 3076
  26.1 5.2 %copy-start.7 = (f32[128]{0:T(128)S(1)}, f32[128]{0:T(128)}, u32[]{:S(2)}) copy-start(f32[128]{0:T(128)} %param.14) | copy-start | bytes 1540
  29.8 2.3 %copy-start.11 = (f32[1,16,128]{2,1,0:T(8,128)S(1)}, f32[1,16,128]{2,1,0:T(8,128)}, u32[]{:S(2)}) copy-start(f32[1,16,128]{2,1,0:T(8,128)} %param.13) | copy-start | bytes 24580
  30.0 2.1 %copy-start.2 = (bf16[128,2,8,128,1]{0,3,2,4,1:T(8,128)(2,1)S(1)}, bf16[128,2,8,128,1]{0,3,2,4,1:T(8,128)(2,1)}, u32[]{:S(2)}) copy-start(bf16[128,2,8,128,1]{0,3,2,4,1:T(8,128)(2,1)} %copy.137) | copy-start | bytes 1572868
  32.1 1.1 %copy-start.3 = (bf16[128,2,8,128,1]{0,3,2,4,1:T(8,128)(2,1)S(1)}, bf16[128,2,8,128,1]{0,3,2,4,1:T(8,128)(2,1)}, u32[]{:S(2)}) copy-start(bf16[128,2,8,128,1]{0,3,2,4,1:T(8,128)(2,1)} %copy.137) | copy-start | bytes 1572868
  32.1 1.1 %copy-start.5 = (bf16[4,128,2,128]{3,2,1,0:T(2,128)(2,1)S(1)}, bf16[4,128,2,128]{3,2,1,0:T(2,128)(2,1)}, u32[]{:S(2)}) copy-start(bf16[4,128,2,128]{3,2,1,0:T(2,128)(2,1)} %squeeze.19) | copy-start | bytes 786436
  36.2 16.8 %all-to-all-start = ((bf16[4,128,512]{1,2,0:T(8,128)(2,1)}), bf16[4,128,512]{1,2,0:T(8,128)(2,1)}, u32[]{:S(2)}, u32[]{:S(2)}) async-start(bf16[4,128,512]{1,2,0:T(8,128)(2,1)} %pad_maximum_fusion), calls=%async_computation | async-start | bytes 1048576 | tf_op jit(solution)/shard_map/all_to_all | solution.py:117
  47.5 2.2 %copy-start = (bf16[1,128,2048]{2,1,0:T(8,128)(2,1)S(1)}, bf16[1,128,2048]{2,1,0:T(8,128)(2,1)}, u32[]{:S(2)}) copy-start(bf16[1,128,2048]{2,1,0:T(8,128)(2,1)} %param.8) | copy-start | bytes 1572868
  49.5 4.8 %copy-start.4 = (f32[128,2,128]{0,2,1:T(8,128)S(1)}, f32[128,2,128]{0,2,1:T(8,128)}, u32[]{:S(2)}) copy-start(f32[128,2,128]{0,2,1:T(8,128)} %get-tuple-element.54) | copy-start | bytes 393220
  49.5 4.8 %copy-start.10 = (f32[128]{0:T(128)S(1)}, f32[128]{0:T(128)}, u32[]{:S(2)}) copy-start(f32[128]{0:T(128)} %param.15) | copy-start | bytes 1540
  49.5 4.9 %copy-start.9 = (f32[256]{0:T(256)S(1)}, f32[256]{0:T(256)}, u32[]{:S(2)}) copy-start(f32[256]{0:T(256)} %copy-done.8) | copy-start | bytes 3076
where the time goes:
time: 98.1 us; the launch traced here: 97.5 us
  blocking collectives  60.3 us (61%)
  other arithmetic  13.2 us (13%)
  local copies, waits for them, and re-layouts  13 us (13%)
  matrix products  5.96 us (6%)
  starting transfers between devices  4.13 us (4%)
    psum x1, blocking collectives, local(): summed_gains = lax.psum(jnp.stack([q_sum, k_sum]), ('ctx', 'head', 'dp'))  40.9 us
    all_gather x1, blocking collectives, local(): lax.all_gather(k_flat, 'ctx', axis=0, tiled=True)  10.4 us
    all_gather x1, blocking collectives, local(): lax.all_gather(v_flat, 'ctx', axis=0, tiled=True)  8.97 us
    all_to_all x1, starting transfers between devices, local(): lax.all_to_all(terms.reshape(block_count, rows, 2 * kv_width), 'ctx', spl...  4.13 us
    unnamed x30, local copies, waits for them, and re-layouts  4.02 us
    reduce_sum x4, other arithmetic, norm_back(): return (grad_raw, jnp.sum(grad_norm * unit_rows, axis=(0, 1)))  3.43 us
    mul x4, local copies, waits for them, and re-layouts, normalize(): unit_rows = values * inverse  2.87 us
    reduce_sum x1, other arithmetic, key_step(): return (running + jnp.sum(query_part, axis=0), (key_part, value_part))  2.06 us
  transfers between devices with their start and end apart: 1, of which 0 were waited for; matrix products, arithmetic and copies ran while one was open for 13% of the time, Pallas kernels for 0%

commit v1 on v0

v1 whole, which is shorter than its diff:
```python
import functools
import math

import jax
import jax.numpy as jnp
from jax import lax
from jax.experimental import pallas as pl
from jax.experimental.pallas import tpu as pltpu
from jax.sharding import PartitionSpec as P

HD = 128
F32 = jnp.float32
BF16 = jnp.bfloat16
MESH = pl.DeviceIdType.MESH
LOG2E = math.log2(math.e)


def dot(a, b):
    return jnp.dot(a, b, preferred_element_type=F32)


def kernel(
    n_ctx, n_head, n_dp, gain_scale,
    q_hbm, k_hbm, v_hbm, o_hbm, g_hbm, lt_hbm, qg_hbm, kg_hbm,
    gq_ref, gk_ref, gv_ref, gain_ref,
    q_v, o_v, g_v, lt_v, qg_v, kg_v,
    kbuf, vbuf, part_out, part_in,
    unit_t, inv_s, qn_t, qn_s, g_t, delta_s, lt2_s, dq_t, gcol_s, ksum_s, buf_a, buf_b,
    in_sem, kv_send, kv_recv, p_send, p_recv, a_send, a_recv, b_send, b_recv,
):
    rows, width = q_v.shape
    heads = width // HD
    kv_width = k_hbm.shape[1]
    kv_count = kv_width // HD
    group = heads // kv_count
    chunk = math.gcd(group, 2)
    scale = 1.0 / math.sqrt(HD)
    me = lax.axis_index("ctx")
    my_head = lax.axis_index("head")
    my_dp = lax.axis_index("dp")
    n_plane = n_ctx * n_head
    my_plane = me * n_head + my_head

    loads = [
        pltpu.make_async_copy(src, dst, in_sem.at[i])
        for i, (src, dst) in enumerate(
            [
                (k_hbm, kbuf.at[me]), (v_hbm, vbuf.at[me]), (lt_hbm, lt_v), (qg_hbm, qg_v),
                (kg_hbm, kg_v), (q_hbm, q_v), (g_hbm, g_v), (o_hbm, o_v),
            ]
        )
    ]
    for load in loads:
        load.start()

    def plane_id(t):
        p = lax.rem(my_plane + t, n_plane)
        return p, {"ctx": p // n_head, "head": lax.rem(p, n_head)}

    barrier = pltpu.get_barrier_semaphore()
    for t in range(1, n_plane):
        pl.semaphore_signal(barrier, inc=1, device_id=plane_id(t)[1], device_id_type=MESH)
    for t in range(1, n_dp):
        pl.semaphore_signal(
            barrier, inc=1, device_id={"dp": lax.rem(my_dp + t, n_dp)}, device_id_type=MESH
        )
    pl.semaphore_wait(barrier, n_plane + n_dp - 2)

    def kv_copy(which, slot, other):
        return pltpu.make_async_remote_copy(
            src_ref=(k_hbm, v_hbm)[which],
            dst_ref=(kbuf, vbuf)[which].at[slot],
            send_sem=kv_send.at[which, other],
            recv_sem=kv_recv.at[which, slot],
            device_id={"ctx": other},
            device_id_type=MESH,
        )

    def part_copy(src, slot, other):
        return pltpu.make_async_remote_copy(
            src_ref=part_out.at[src],
            dst_ref=part_in.at[slot],
            send_sem=p_send.at[src],
            recv_sem=p_recv.at[slot],
            device_id={"ctx": other},
            device_id_type=MESH,
        )

    for t in range(1, n_ctx):
        @pl.when(me + t < n_ctx)
        def _():
            kv_copy(0, me, me + t).start()
            kv_copy(1, me, me + t).start()

    for load in loads:
        load.wait()

    gcol_s[...] = jnp.broadcast_to(qg_v[...], (HD, HD)).T
    for h in range(heads):
        hs = slice(h * HD, (h + 1) * HD)
        q_h = q_v[:, hs].T.astype(F32)
        inv = lax.rsqrt(jnp.mean(q_h * q_h, axis=0, keepdims=True) + 1e-06)
        unit = q_h * inv
        norm = (unit * gcol_s[...]).astype(BF16)
        unit_t[:, hs] = unit
        inv_s[:, hs] = inv
        qn_t[:, hs] = norm
        qn_s[h * rows:(h + 1) * rows, :] = norm.T
        gt = g_v[:, hs].T
        g_t[:, hs] = gt
        delta_s[:, hs] = jnp.sum(gt.astype(F32) * o_v[:, hs].T.astype(F32), axis=0, keepdims=True)
        lt2_s[:, hs] = lt_v[h:h + 1, :] * LOG2E

    def k_parts(b, c):
        x = kbuf[b, :, c * HD:(c + 1) * HD].astype(F32)
        inv = lax.rsqrt(jnp.mean(x * x, axis=-1, keepdims=True) + 1e-06)
        return x * inv, inv

    def block(b, diagonal):
        ksum = jnp.zeros((1, HD), F32)
        for c in range(kv_count):
            cs = slice(c * HD, (c + 1) * HD)
            k_unit, _ = k_parts(b, c)
            kn = (k_unit * kg_v[...]).astype(BF16)
            kn_t = kn.T
            vv = vbuf[b, :, cs]
            dk = jnp.zeros((rows, HD), F32)
            dv = jnp.zeros((rows, HD), F32)
            if diagonal:
                key_pos = lax.broadcasted_iota(jnp.int32, (rows, chunk * rows), 0)
                query_pos = lax.rem(
                    lax.broadcasted_iota(jnp.int32, (rows, chunk * rows), 1), rows
                )
                causal = query_pos >= key_pos
            for j in range(group // chunk):
                h = c * group + j * chunk
                sl = slice(h * HD, (h + chunk) * HD)
                s = dot(kn, qn_t[:, sl])
                p = jnp.exp2(s * (scale * LOG2E) - lt2_s[:, sl])
                if diagonal:
                    p = jnp.where(causal, p, 0.0)
                dp = dot(vv, g_t[:, sl])
                ds = (p * (dp - delta_s[:, sl])).astype(BF16)
                g_nat = jnp.concatenate(
                    [g_v[:, (h + i) * HD:(h + i + 1) * HD] for i in range(chunk)], axis=0
                )
                dv += dot(p.astype(BF16), g_nat)
                dk += dot(ds, qn_s[h * rows:(h + chunk) * rows, :])
                dq = dot(kn_t, ds)
                if diagonal:
                    dq_t[:, sl] = dq
                else:
                    dq_t[:, sl] += dq
            dk = dk * scale
            ksum += jnp.sum(dk * k_unit, axis=0, keepdims=True)
            if diagonal:
                gk_ref[:, cs] = dk
                gv_ref[:, cs] = dv
            else:
                part_out[b, :, cs] = dk.astype(BF16)
                part_out[b, :, kv_width + c * HD:kv_width + (c + 1) * HD] = dv.astype(BF16)
        return ksum

    ksum_s[...] = block(me, True)

    def step(t, carry):
        b = me - 1 - t
        kv_copy(0, b, b).wait_recv()
        kv_copy(1, b, b).wait_recv()
        ksum_s[...] += block(b, False)
        part_copy(b, me, b).start()
        return carry

    lax.fori_loop(0, me, step, 0)

    q_acc = jnp.zeros((HD, rows), F32)
    for h in range(heads):
        hs = slice(h * HD, (h + 1) * HD)
        gn = dq_t[:, hs] * scale
        unit = unit_t[:, hs]
        q_acc += gn * unit
        gp = gn * gcol_s[...]
        mean = jnp.mean(gp * unit, axis=0, keepdims=True)
        gq_ref[:, hs] = ((gp - unit * mean) * inv_s[:, hs]).T

    def gain_copy(buf, slot, send_sem, recv_sem, device_id):
        return pltpu.make_async_remote_copy(
            src_ref=buf.at[slot],
            dst_ref=buf.at[slot],
            send_sem=send_sem,
            recv_sem=recv_sem.at[slot],
            device_id=device_id,
            device_id_type=MESH,
        )

    buf_a[my_dp] = jnp.concatenate(
        [
            jnp.sum(q_acc.T, axis=0, keepdims=True), ksum_s[...],
            jnp.zeros((6, HD), F32),
        ],
        axis=0,
    )
    sent_a = []
    for t in range(1, n_dp):
        other = lax.rem(my_dp + t, n_dp)
        copy = gain_copy(buf_a, my_dp, a_send.at[t], a_recv, {"dp": other})
        copy.start()
        sent_a.append(copy)
    for t in range(1, n_dp):
        other = lax.rem(my_dp + t, n_dp)
        gain_copy(buf_a, other, a_send.at[t], a_recv, {"dp": other}).wait_recv()
    buf_b[my_plane] = jnp.sum(buf_a[...], axis=0)
    sent_b = []
    for t in range(1, n_plane):
        copy = gain_copy(buf_b, my_plane, b_send.at[t], b_recv, plane_id(t)[1])
        copy.start()
        sent_b.append(copy)

    def add_parts(a, carry):
        part_copy(a, a, a).wait_recv()
        gk_ref[...] += part_in[a, :, :kv_width].astype(F32)
        gv_ref[...] += part_in[a, :, kv_width:].astype(F32)
        return carry

    lax.fori_loop(me + 1, n_ctx, add_parts, 0)
    for c in range(kv_count):
        cs = slice(c * HD, (c + 1) * HD)
        unit, inv = k_parts(me, c)
        gp = gk_ref[:, cs] * kg_v[...]
        gk_ref[:, cs] = (gp - unit * jnp.mean(gp * unit, axis=-1, keepdims=True)) * inv

    for t in range(1, n_plane):
        slot, device_id = plane_id(t)
        gain_copy(buf_b, slot, b_send.at[t], b_recv, device_id).wait_recv()
    gain_ref[...] = jnp.sum(buf_b[...], axis=0)[:2] * gain_scale

    for copy in sent_a + sent_b:
        copy.wait_send()
    for t in range(1, n_ctx):
        @pl.when(me + t < n_ctx)
        def _():
            kv_copy(0, me, me + t).wait_send()
            kv_copy(1, me, me + t).wait_send()

        @pl.when(me - t >= 0)
        def _():
            part_copy(me - t, me, me - t).wait_send()


def local(query_raw, key_raw, value_rows, attn_out, out_grad, log_totals, query_gain, key_gain):
    n_ctx = lax.axis_size("ctx")
    n_head = lax.axis_size("head")
    n_dp = lax.axis_size("dp")
    batch, rows, width = query_raw.shape
    kv_width = key_raw.shape[2]
    heads = width // HD
    n_plane = n_ctx * n_head
    pair_count = batch * n_dp * rows * n_ctx * heads * n_head
    vmem = pltpu.VMEM
    dma = pltpu.SemaphoreType.DMA
    flops = 10 * heads * rows * rows * HD * n_ctx
    gq, gk, gv, gains = pl.pallas_call(
        functools.partial(kernel, n_ctx, n_head, n_dp, 1.0 / math.sqrt(pair_count)),
        out_shape=(
            jax.ShapeDtypeStruct((rows, width), F32),
            jax.ShapeDtypeStruct((rows, kv_width), F32),
            jax.ShapeDtypeStruct((rows, kv_width), F32),
            jax.ShapeDtypeStruct((2, HD), F32),
        ),
        in_specs=[pl.BlockSpec(memory_space=pl.ANY)] * 8,
        out_specs=tuple([pl.BlockSpec(memory_space=pltpu.VMEM)] * 4),
        scratch_shapes=[
            vmem((rows, width), BF16), vmem((rows, width), BF16), vmem((rows, width), BF16),
            vmem((heads, rows), F32), vmem((1, HD), F32), vmem((1, HD), F32),
            vmem((n_ctx, rows, kv_width), BF16), vmem((n_ctx, rows, kv_width), BF16),
            vmem((n_ctx, rows, 2 * kv_width), BF16), vmem((n_ctx, rows, 2 * kv_width), BF16),
            vmem((HD, heads * rows), F32), vmem((1, heads * rows), F32),
            vmem((HD, heads * rows), BF16), vmem((heads * rows, HD), BF16),
            vmem((HD, heads * rows), BF16), vmem((1, heads * rows), F32),
            vmem((1, heads * rows), F32), vmem((HD, heads * rows), F32),
            vmem((HD, HD), F32), vmem((1, HD), F32),
            vmem((n_dp, 8, HD), F32), vmem((n_plane, 8, HD), F32),
            dma((8,)), dma((2, n_ctx)), dma((2, n_ctx)), dma((n_ctx,)), dma((n_ctx,)),
            dma((n_dp,)), dma((n_dp,)), dma((n_plane,)), dma((n_plane,)),
        ],
        compiler_params=pltpu.CompilerParams(
            collective_id=0, has_side_effects=True, vmem_limit_bytes=32 * 1024 * 1024
        ),
        cost_estimate=pl.CostEstimate(
            flops=flops, bytes_accessed=4 * rows * width * 4, transcendentals=heads * rows * rows * n_ctx
        ),
    )(
        query_raw[0], key_raw[0], value_rows[0], attn_out[0], out_grad[0], log_totals[0],
        query_gain.reshape(1, HD), key_gain.reshape(1, HD),
    )
    return gq[None], gk[None], gv[None], gains


def solution(mesh):
    return jax.shard_map(
        local,
        mesh=mesh,
        in_specs=(
            P("dp", "ctx", "head"),
            P("dp", "ctx", "head"),
            P("dp", "ctx", "head"),
            P("dp", "ctx", "head"),
            P("dp", "ctx", "head"),
            P("dp", "head", "ctx"),
            P(),
            P(),
        ),
        out_specs=(P("dp", "ctx", "head"), P("dp", "ctx", "head"), P("dp", "ctx", "head"), P()),
        check_vma=False,
    )
```

time: 98.1 us -> 32.9 us (0.34)
  blocking collectives: 60.3 us -> 0 us
  Pallas kernels: 0 us -> 23.5 us
  other arithmetic: 13.2 us -> 0 us
  matrix products: 5.96 us -> 0 us
  local copies, waits for them, and re-layouts: 13 us -> 8.32 us
  starting transfers between devices: 4.13 us -> 0 us
    psum x1 -> x0, blocking collectives: 40.9 us -> none  [local(): summed_gains = lax.psum(jnp.stack([q_sum, k_sum]), ('ctx', 'head', 'dp'))]
    pallas_call x0 -> x1, Pallas kernels: none -> 23.5 us  [local(): pl.pallas_call(functools.partial(kernel, n_ctx, n_head, n_dp, 1.0 / math....]
    all_gather x2 -> x0, blocking collectives: 19.4 us -> none  [the longest x1 10.4 us: local(): lax.all_gather(k_flat, 'ctx', axis=0, tiled=True)]
    reduce_sum x10 -> x0, other arithmetic: 8.01 us -> none  [the longest x4 3.43 us: norm_back(): return (grad_raw, jnp.sum(grad_norm * unit_rows, axis=(0, 1)))]
    dot_general x5 -> x0, matrix products: 5.96 us -> none  [the longest x1 2.05 us: key_step(): jnp.einsum('cgqpk,pkcd->pqcgd', score_gradient, key_group, preferred_elem...]
    unnamed x30 -> x20, local copies, waits for them, and re-layouts: 4.02 us -> 8.32 us
    all_to_all x1 -> x0, starting transfers between devices: 4.13 us -> none  [local(): lax.all_to_all(terms.reshape(block_count, rows, 2 * kv_width), 'ctx', spl...]
    mul x8 -> x0, local copies, waits for them, and re-layouts: 4.02 us -> none  [the longest x4 2.87 us: normalize(): unit_rows = values * inverse]
  transfers between devices with their start and end apart: 1 -> 0, of which waited for: 0 -> 0; matrix products, arithmetic and copies ran while one was open for 13% -> 0% of each run, Pallas kernels for 0% -> 0%
where the time goes in v1:
time: 32.9 us; the launch traced here: 32.5 us
  Pallas kernels  23.5 us (71%)
  local copies, waits for them, and re-layouts  8.32 us (25%)
  between operations  0.67 us (2%)
    pallas_call x1, Pallas kernels, local(): pl.pallas_call(functools.partial(kernel, n_ctx, n_head, n_dp, 1.0 / math....  23.5 us
    unnamed x20, local copies, waits for them, and re-layouts  8.32 us

profile of v1, /device:TPU:0, one launch (start us, length us, event | category | flops | bytes accessed | tf_op | source)
XLA Modules:
  0.0 32.5 jit_solution(7316445588541196589)
XLA Ops:
  0.6 0.0 copy-start.5
  0.6 0.0 copy-start.6
  0.7 0.0 copy-start.7
  0.7 0.7 %copy-done.5 = f32[1,16,128]{2,1,0:T(8,128)S(1)} copy-done((f32[1,16,128]{2,1,0:T(8,128)S(1)}, f32[1,16,128]{2,1,0:T(8,128)}, u32[]{:S(2)}) %copy-start.5) | copy-done | bytes 8216
  1.3 0.0 copy-done.6
  1.3 0.0 copy-done.7
  1.3 0.0 copy-start
  1.3 1.0 %copy-done = bf16[1,128,2048]{2,1,0:T(8,128)(2,1)S(1)} copy-done((bf16[1,128,2048]{2,1,0:T(8,128)(2,1)S(1)}, bf16[1,128,2048]{2,1,0:T(8,128)(2,1)}, u32[]{:S(2)}) %copy-start) | copy-done | bytes 524312
  2.4 0.0 copy-start.1
  2.4 1.0 %copy-done.1 = bf16[1,128,2048]{2,1,0:T(8,128)(2,1)S(1)} copy-done((bf16[1,128,2048]{2,1,0:T(8,128)(2,1)S(1)}, bf16[1,128,2048]{2,1,0:T(8,128)(2,1)}, u32[]{:S(2)}) %copy-start.1) | copy-done | bytes 524312
  3.4 0.0 copy-start.2
  3.4 1.0 %copy-done.2 = bf16[1,128,2048]{2,1,0:T(8,128)(2,1)S(1)} copy-done((bf16[1,128,2048]{2,1,0:T(8,128)(2,1)S(1)}, bf16[1,128,2048]{2,1,0:T(8,128)(2,1)}, u32[]{:S(2)}) %copy-start.2) | copy-done | bytes 524312
  4.5 0.0 copy-start.3
  4.5 0.8 %copy-done.3 = bf16[1,128,256]{2,1,0:T(8,128)(2,1)S(1)} copy-done((bf16[1,128,256]{2,1,0:T(8,128)(2,1)S(1)}, bf16[1,128,256]{2,1,0:T(8,128)(2,1)}, u32[]{:S(2)}) %copy-start.3) | copy-done | bytes 65560
  5.3 0.0 copy-start.4
  5.3 0.8 %copy-done.4 = bf16[1,128,256]{2,1,0:T(8,128)(2,1)S(1)} copy-done((bf16[1,128,256]{2,1,0:T(8,128)(2,1)S(1)}, bf16[1,128,256]{2,1,0:T(8,128)(2,1)}, u32[]{:S(2)}) %copy-start.4) | copy-done | bytes 65560
  6.1 23.5 %shard_map.111 = (f32[128,2048]{1,0:T(8,128)S(1)}, f32[128,256]{1,0:T(8,128)S(1)}, f32[128,256]{1,0:T(8,128)S(1)}, f32[2,128]{1,0:T(2,128)S(1)}) custom-call(bf16[128,2048]{1,0:T(8,128)(2,1)S(1)} %bitcast.14, bf16[128,256]{1,0:T(8,128)(2,1)S(1)} %bitcast.17, bf16[128,256]{1,0:T(8,128)(2,1)S(1)} %bitcast.18, bf16[128,2048]{1,0:T(8,128)(2,1)S(1)} %bitcast.15, ...), custom_call_target="tpu_custom_call" | custom-call | flops 1342177280 | bytes 4194304 | tf_op jit(solution)/shard_map/pallas_call | solution.py:262
  29.6 1.0 %copy.16 = f32[1,128,2048]{2,1,0:T(8,128)} copy(f32[1,128,2048]{2,1,0:T(8,128)S(1)} %bitcast.11) | data formatting | bytes 2097152
  30.6 0.7 %copy.17 = f32[1,128,256]{2,1,0:T(8,128)} copy(f32[1,128,256]{2,1,0:T(8,128)S(1)} %bitcast.13) | data formatting | bytes 262144
  31.3 0.7 %copy.18 = f32[1,128,256]{2,1,0:T(8,128)} copy(f32[1,128,256]{2,1,0:T(8,128)S(1)} %bitcast.12) | data formatting | bytes 262144
  31.9 0.6 %copy.19 = f32[2,128]{1,0:T(2,128)} copy(f32[2,128]{1,0:T(2,128)S(1)} %get-tuple-element.19) | data formatting | bytes 2048
Async XLA Ops:
  0.6 0.7 %copy-start.5 = (f32[1,16,128]{2,1,0:T(8,128)S(1)}, f32[1,16,128]{2,1,0:T(8,128)}, u32[]{:S(2)}) copy-start(f32[1,16,128]{2,1,0:T(8,128)} %param.13) | copy-start | bytes 24580
  0.6 0.7 %copy-start.6 = (f32[128]{0:T(128)S(1)}, f32[128]{0:T(128)}, u32[]{:S(2)}) copy-start(f32[128]{0:T(128)} %param.14) | copy-start | bytes 1540
  0.7 0.7 %copy-start.7 = (f32[128]{0:T(128)S(1)}, f32[128]{0:T(128)}, u32[]{:S(2)}) copy-start(f32[128]{0:T(128)} %param.15) | copy-start | bytes 1540
  1.3 1.0 %copy-start = (bf16[1,128,2048]{2,1,0:T(8,128)(2,1)S(1)}, bf16[1,128,2048]{2,1,0:T(8,128)(2,1)}, u32[]{:S(2)}) copy-start(bf16[1,128,2048]{2,1,0:T(8,128)(2,1)} %param.8) | copy-start | bytes 1572868
  2.4 1.0 %copy-start.1 = (bf16[1,128,2048]{2,1,0:T(8,128)(2,1)S(1)}, bf16[1,128,2048]{2,1,0:T(8,128)(2,1)}, u32[]{:S(2)}) copy-start(bf16[1,128,2048]{2,1,0:T(8,128)(2,1)} %param.11) | copy-start | bytes 1572868
  3.4 1.0 %copy-start.2 = (bf16[1,128,2048]{2,1,0:T(8,128)(2,1)S(1)}, bf16[1,128,2048]{2,1,0:T(8,128)(2,1)}, u32[]{:S(2)}) copy-start(bf16[1,128,2048]{2,1,0:T(8,128)(2,1)} %param.12) | copy-start | bytes 1572868
  4.5 0.8 %copy-start.3 = (bf16[1,128,256]{2,1,0:T(8,128)(2,1)S(1)}, bf16[1,128,256]{2,1,0:T(8,128)(2,1)}, u32[]{:S(2)}) copy-start(bf16[1,128,256]{2,1,0:T(8,128)(2,1)} %param.9) | copy-start | bytes 196612
  5.3 0.8 %copy-start.4 = (bf16[1,128,256]{2,1,0:T(8,128)(2,1)S(1)}, bf16[1,128,256]{2,1,0:T(8,128)(2,1)}, u32[]{:S(2)}) copy-start(bf16[1,128,256]{2,1,0:T(8,128)(2,1)} %param.10) | copy-start | bytes 196612

commit v2 on v1

--- a/solution.py
+++ b/solution.py
@@ -247,6 +247,27 @@
             part_copy(me - t, me, me - t).wait_send()
 
 
+def hold(*xs):
+    return [pltpu.with_memory_space_constraint(x, pltpu.HBM) for x in xs]
+
+
+def write_out(*refs):
+    sem = refs[-1]
+    half = len(refs) // 2
+    copies = []
+    for i, (src, dst) in enumerate(zip(refs[:half], refs[half:-1])):
+        rows = src.shape[0]
+        cuts = 4 if rows % 64 == 0 and src.shape[1] > 512 else 1
+        step = rows // cuts
+        for c in range(cuts):
+            part = pl.ds(c * step, step)
+            copies.append(pltpu.make_async_copy(src.at[part], dst.at[part], sem.at[len(copies)]))
+    for copy in copies:
+        copy.start()
+    for copy in copies:
+        copy.wait()
+
+
 def local(query_raw, key_raw, value_rows, attn_out, out_grad, log_totals, query_gain, key_gain):
     n_ctx = lax.axis_size("ctx")
     n_head = lax.axis_size("head")
@@ -267,7 +288,7 @@
             jax.ShapeDtypeStruct((rows, kv_width), F32),
             jax.ShapeDtypeStruct((2, HD), F32),
         ),
-        in_specs=[pl.BlockSpec(memory_space=pl.ANY)] * 8,
+        in_specs=[pl.BlockSpec(memory_space=pltpu.HBM)] * 8,
         out_specs=tuple([pl.BlockSpec(memory_space=pltpu.VMEM)] * 4),
         scratch_shapes=[
             vmem((rows, width), BF16), vmem((rows, width), BF16), vmem((rows, width), BF16),
@@ -284,15 +305,24 @@
             dma((n_dp,)), dma((n_dp,)), dma((n_plane,)), dma((n_plane,)),
         ],
         compiler_params=pltpu.CompilerParams(
-            collective_id=0, has_side_effects=True, vmem_limit_bytes=32 * 1024 * 1024
+            collective_id=0, has_side_effects=True, vmem_limit_bytes=48 * 1024 * 1024
         ),
         cost_estimate=pl.CostEstimate(
             flops=flops, bytes_accessed=4 * rows * width * 4, transcendentals=heads * rows * rows * n_ctx
         ),
-    )(
+    )(*hold(
         query_raw[0], key_raw[0], value_rows[0], attn_out[0], out_grad[0], log_totals[0],
         query_gain.reshape(1, HD), key_gain.reshape(1, HD),
-    )
+    ))
+    results = (gq, gk, gv, gains)
+    gq, gk, gv, gains = pl.pallas_call(
+        write_out,
+        out_shape=tuple(jax.ShapeDtypeStruct(x.shape, x.dtype) for x in results),
+        in_specs=[pl.BlockSpec(memory_space=pl.ANY)] * 4,
+        out_specs=tuple([pl.BlockSpec(memory_space=pl.ANY)] * 4),
+        scratch_shapes=[dma((16,))],
+        compiler_params=pltpu.CompilerParams(vmem_limit_bytes=1024 * 1024),
+    )(*results)
     return gq[None], gk[None], gv[None], gains
 
 

time: 32.9 us -> 25.5 us (0.78)
  local copies, waits for them, and re-layouts: 8.32 us -> 0 us
  Pallas kernels: 23.5 us -> 24.7 us
    unnamed x20 -> x0, local copies, waits for them, and re-layouts: 8.32 us -> none
    pallas_call x0 -> x1, Pallas kernels: none -> 1.19 us  [local(): pl.pallas_call(write_out, out_shape=tuple((jax.ShapeDtypeStruct(x.shape,...]
where the time goes in v2:
time: 25.5 us; the launch traced here: 25.3 us
  Pallas kernels  24.7 us (97%)
  between operations  0.64 us (3%)
    pallas_call x1, Pallas kernels, local(): pl.pallas_call(functools.partial(kernel, n_ctx, n_head, n_dp, 1.0 / math....  23.5 us
    pallas_call x1, Pallas kernels, local(): pl.pallas_call(write_out, out_shape=tuple((jax.ShapeDtypeStruct(x.shape,...  1.19 us

profile of v2, /device:TPU:0, one launch (start us, length us, event | category | flops | bytes accessed | tf_op | source)
XLA Modules:
  0.0 25.3 jit_solution(7540459824907889643)
XLA Ops:
  0.6 23.5 %shard_map.111 = (f32[128,2048]{1,0:T(8,128)S(1)}, f32[128,256]{1,0:T(8,128)S(1)}, f32[128,256]{1,0:T(8,128)S(1)}, f32[2,128]{1,0:T(2,128)S(1)}) custom-call(bf16[128,2048]{1,0:T(8,128)(2,1)} %bitcast.12, bf16[128,256]{1,0:T(8,128)(2,1)} %bitcast.17, bf16[128,256]{1,0:T(8,128)(2,1)} %bitcast.18, bf16[128,2048]{1,0:T(8,128)(2,1)} %bitcast.13, ...), custom_call_target="tpu_custom_call" | custom-call | flops 1342177280 | bytes 4194304 | tf_op jit(solution)/shard_map/pallas_call | solution.py:283
  24.1 1.2 %shard_map.112 = (f32[128,2048]{1,0:T(8,128)}, f32[128,256]{1,0:T(8,128)}, f32[128,256]{1,0:T(8,128)}, f32[2,128]{1,0:T(2,128)}) custom-call(f32[128,2048]{1,0:T(8,128)S(1)} %get-tuple-element.12.refs_0_, f32[128,256]{1,0:T(8,128)S(1)} %get-tuple-element.13.refs_1_, f32[128,256]{1,0:T(8,128)S(1)} %get-tuple-element.14.refs_2_, ...), custom_call_target="tpu_custom_call" | custom-call | tf_op jit(solution)/shard_map/pallas_call | solution.py:318

commit v3 on v2

--- a/solution.py
+++ b/solution.py
@@ -68,7 +68,7 @@
 
     def kv_copy(which, slot, other):
         return pltpu.make_async_remote_copy(
-            src_ref=(k_hbm, v_hbm)[which],
+            src_ref=(kbuf, vbuf)[which].at[slot],
             dst_ref=(kbuf, vbuf)[which].at[slot],
             send_sem=kv_send.at[which, other],
             recv_sem=kv_recv.at[which, slot],
@@ -86,13 +86,14 @@
             device_id_type=MESH,
         )
 
-    for t in range(1, n_ctx):
-        @pl.when(me + t < n_ctx)
-        def _():
-            kv_copy(0, me, me + t).start()
-            kv_copy(1, me, me + t).start()
-
-    for load in loads:
+    for which in range(2):
+        loads[which].wait()
+        for t in range(1, n_ctx):
+            @pl.when(me + t < n_ctx)
+            def _():
+                kv_copy(which, me, me + t).start()
+
+    for load in loads[2:]:
         load.wait()
 
     gcol_s[...] = jnp.broadcast_to(qg_v[...], (HD, HD)).T

time: 25.5 us -> 25.3 us (level)
  no operation moved by 1% of the time
where the time goes in v3:
time: 25.3 us; the launch traced here: 25.1 us
  Pallas kernels  24.5 us (97%)
  between operations  0.64 us (3%)
    pallas_call x1, Pallas kernels, local(): pl.pallas_call(functools.partial(kernel, n_ctx, n_head, n_dp, 1.0 / math....  23.3 us
    pallas_call x1, Pallas kernels, local(): pl.pallas_call(write_out, out_shape=tuple((jax.ShapeDtypeStruct(x.shape,...  1.19 us

profile of v3, /device:TPU:0, one launch (start us, length us, event | category | flops | bytes accessed | tf_op | source)
XLA Modules:
  0.0 25.1 jit_solution(18054467172326497800)
XLA Ops:
  0.6 23.3 %shard_map.111 = (f32[128,2048]{1,0:T(8,128)S(1)}, f32[128,256]{1,0:T(8,128)S(1)}, f32[128,256]{1,0:T(8,128)S(1)}, f32[2,128]{1,0:T(2,128)S(1)}) custom-call(bf16[128,2048]{1,0:T(8,128)(2,1)} %bitcast.12, bf16[128,256]{1,0:T(8,128)(2,1)} %bitcast.17, bf16[128,256]{1,0:T(8,128)(2,1)} %bitcast.18, bf16[128,2048]{1,0:T(8,128)(2,1)} %bitcast.13, ...), custom_call_target="tpu_custom_call" | custom-call | flops 1342177280 | bytes 4194304 | tf_op jit(solution)/shard_map/pallas_call | solution.py:284
  23.9 1.2 %shard_map.112 = (f32[128,2048]{1,0:T(8,128)}, f32[128,256]{1,0:T(8,128)}, f32[128,256]{1,0:T(8,128)}, f32[2,128]{1,0:T(2,128)}) custom-call(f32[128,2048]{1,0:T(8,128)S(1)} %get-tuple-element.12.refs_0_, f32[128,256]{1,0:T(8,128)S(1)} %get-tuple-element.13.refs_1_, f32[128,256]{1,0:T(8,128)S(1)} %get-tuple-element.14.refs_2_, ...), custom_call_target="tpu_custom_call" | custom-call | tf_op jit(solution)/shard_map/pallas_call | solution.py:319
